TPU v7x, 512 devices: a whole 4x8x8 slice. The times are simulated.
512 devices in a mesh: sec: 8 (over y), rad: 16 (over z, x_hi), ax: 4 (over x_lo, core).
Axes of the slice: x: 4 (x_hi: 2, x_lo: 2; x = x_hi * 2 + x_lo), y: 8, z: 8, core: 2. Of those that a mesh axis runs over, the one named last changes fastest.
Arguments:
- state: float32 [5, 8, 1024, 2048], P(None, 'ax', 'rad', 'sec'), may hold values from -1.6 to 4, as said below
- coarsen: int32 [16], replicated, may hold values from 1 to 16, as said below
Outputs:
- tendency: float32 [5, 8, 1024, 2048], P(None, 'ax', 'rad', 'sec')
Inputs may be any that keep to these rules, and one draw needn't show every extreme that they name: `coarsen`: each entry is a power of two; cycle 0 takes 16 and cycle 16 - 1 takes 1. state[0] (density) lies in 0.6 to 1.4, the momenta in -1.6 to 1.6, state[4] (energy) in 2.5 to 4.0.
All inputs are finite; a program needn't handle non-finite values.
Results may differ from a plain program's by a relative error of at most 0.0003.
Values sent between devices are 32-bit elements; how exact they have to be, the bound alone decides.
A program may use at most 64 MiB of HBM per device.

v0:
```python
import math
import jax
import jax.numpy as jnp
from jax import lax
from jax.sharding import PartitionSpec as P

R_NEAR = 16
GAMMA = 1.4
KAPPA = 1.44


def padded_2(value, sides, width):
    for axis, dim in sides:
        size, length = (lax.axis_size(axis), value.shape[dim])
        up = [(i, (i + 1) % size) for i in range(size)]
        down = [(j, i) for i, j in up]
        last = lax.slice_in_dim(value, length - width, length, axis=dim)
        first = lax.slice_in_dim(value, 0, width, axis=dim)
        before = lax.ppermute(last, axis, up)
        after = lax.ppermute(first, axis, down)
        value = jnp.concatenate([before, value, after], axis=dim)
    return value


def spread(value, axis, root):
    mine = lax.axis_index(axis) == root
    return lax.psum(jnp.where(mine, value, jnp.zeros_like(value)), axis)


def body(state, coarsen):
    fields, planes, cycles_dev, cells_dev = state.shape
    sec_count = lax.axis_size("sec")
    rad_count = lax.axis_size("rad")
    ax_count = lax.axis_size("ax")
    sec_index = lax.axis_index("sec")
    rad_index = lax.axis_index("rad")
    ax_index = lax.axis_index("ax")
    total_cells = cells_dev * sec_count
    dtheta = 2.0 * math.pi / total_cells
    padded = padded_2(state, (("sec", 3), ("rad", 2), ("ax", 1)), 1)
    plane_pos = ax_index * planes + jnp.arange(-1, planes + 1, dtype=jnp.int32)
    cycle_pos = rad_index * cycles_dev + jnp.arange(-1, cycles_dev + 1, dtype=jnp.int32)
    inside_ax = ((plane_pos >= 0) & (plane_pos < planes * ax_count)).astype(jnp.float32)
    inside_rad = ((cycle_pos >= 0) & (cycle_pos < cycles_dev * rad_count)).astype(jnp.float32)
    ghost_plane = jnp.arange(planes + 2) % (planes + 1) == 0
    ghost_cycle = jnp.arange(cycles_dev + 2) % (cycles_dev + 1) == 0
    ghost_cell = jnp.arange(cells_dev + 2) % (cells_dev + 1) == 0
    ghosts = (
        ghost_plane.astype(jnp.int32)[:, None, None]
        + ghost_cycle.astype(jnp.int32)[None, :, None]
        + ghost_cell.astype(jnp.int32)[None, None, :]
    )
    corner = ghosts >= 2
    density = jnp.where(corner, 1.0, padded[0])
    mom_ax = padded[1]
    mom_rad = padded[2]
    mom_az = padded[3]
    energy = padded[4]
    vel_ax = mom_ax / density
    vel_rad = mom_rad / density
    vel_az = mom_az / density
    pressure = (GAMMA - 1.0) * (
        energy - 0.5 * (mom_ax * vel_ax + mom_rad * vel_rad + mom_az * vel_az)
    )
    radius_pad = cycle_pos.astype(jnp.float32) + 0.5
    flux_ax = jnp.stack(
        [
            mom_ax,
            mom_ax * vel_ax + pressure,
            mom_rad * vel_ax,
            mom_az * vel_ax,
            (energy + pressure) * vel_ax,
        ]
    )
    flux_ax = flux_ax * inside_ax[None, :, None, None]
    flux_rad = jnp.stack(
        [
            mom_rad,
            mom_ax * vel_rad,
            mom_rad * vel_rad + pressure,
            mom_az * vel_rad,
            (energy + pressure) * vel_rad,
        ]
    )
    flux_rad = flux_rad * (radius_pad * inside_rad)[None, None, :, None]
    flux_az = jnp.stack(
        [
            mom_az,
            mom_ax * vel_az,
            mom_rad * vel_az,
            mom_az * vel_az + pressure,
            (energy + pressure) * vel_az,
        ]
    )
    radius = radius_pad[1:-1][:, None]
    tendency = -(flux_ax[:, 2:, 1:-1, 1:-1] - flux_ax[:, :-2, 1:-1, 1:-1]) * 0.5
    tendency = (
        tendency - (flux_rad[:, 1:-1, 2:, 1:-1] - flux_rad[:, 1:-1, :-2, 1:-1]) * 0.5 / radius
    )
    tendency = tendency - (flux_az[:, 1:-1, 1:-1, 2:] - flux_az[:, 1:-1, 1:-1, :-2]) * 0.5 / (
        radius * dtheta
    )
    inner_press = pressure[1:-1, 1:-1, 1:-1]
    inner_mom_az = mom_az[1:-1, 1:-1, 1:-1]
    inner_mom_rad = mom_rad[1:-1, 1:-1, 1:-1]
    inner_vel_az = vel_az[1:-1, 1:-1, 1:-1]
    zero_part = jnp.zeros_like(inner_press)
    source = jnp.stack(
        [
            zero_part,
            zero_part,
            (inner_press + inner_mom_az * inner_vel_az) / radius,
            -(inner_mom_rad * inner_vel_az) / radius,
            zero_part,
        ]
    )
    tendency = tendency + source
    own_pos = sec_index * cells_dev + jnp.arange(cells_dev, dtype=jnp.int32)

    def kernel(cycle_factor, cycle_blocks, log_ratio, scale_const, columns):
        rows_coarse = own_pos // cycle_factor
        columns_coarse = columns // cycle_factor
        distance = ((rows_coarse[:, None] - columns_coarse[None, :]) % cycle_blocks).astype(
            jnp.float32
        )
        blocks_f = cycle_blocks.astype(jnp.float32)
        return (jnp.exp(distance * log_ratio) + jnp.exp((blocks_f - distance) * log_ratio)) / (
            scale_const * cycle_factor.astype(jnp.float32)
        )

    near_axis = tendency[:, :, :R_NEAR, :]
    cycle_lines = jnp.transpose(near_axis, (2, 0, 1, 3)).reshape(R_NEAR, fields * planes, cells_dev)
    shared = spread(cycle_lines, "rad", 0)
    per_device = R_NEAR // rad_count
    my_cycles = lax.dynamic_slice_in_dim(shared, rad_index * per_device, per_device, 0)
    selector = (rad_index * per_device + jnp.arange(per_device, dtype=jnp.int32))[
        :, None
    ] == jnp.arange(coarsen.shape[0], dtype=jnp.int32)[None, :]
    factor = jnp.sum(jnp.where(selector, coarsen[None, :], 0), axis=1)
    blocks = total_cells // factor
    factor_f = factor.astype(jnp.float32)
    stiffness = KAPPA / (factor_f * dtheta) ** 2
    inverse_half = 0.5 / stiffness
    one_minus = jnp.sqrt(inverse_half * (2.0 + inverse_half)) - inverse_half
    log_ratio = jnp.log1p(-one_minus)
    scale_const = (
        stiffness
        * one_minus
        * (2.0 - one_minus)
        / (1.0 - one_minus)
        * -jnp.expm1(blocks.astype(jnp.float32) * log_ratio)
    )
    portion = lax.all_gather(my_cycles, "sec", axis=2, tiled=True)
    columns = jnp.arange(portion.shape[2], dtype=jnp.int32)

    def per_cycle(cycle_item):
        lines_one, cycle_factor, cycle_blocks, cycle_log, cycle_scale = cycle_item
        table = kernel(cycle_factor, cycle_blocks, cycle_log, cycle_scale, columns)
        return jnp.einsum("lq,pq->lp", lines_one, table, precision=lax.Precision.HIGHEST)

    smoothed = lax.map(per_cycle, (portion, factor, blocks, log_ratio, scale_const))
    result = lax.all_gather(smoothed, "rad", axis=0, tiled=True)
    restored = jnp.transpose(result.reshape(R_NEAR, fields, planes, cells_dev), (1, 2, 0, 3))
    near_new = jnp.where(rad_index == 0, restored, near_axis)
    return jnp.concatenate([near_new, tendency[:, :, R_NEAR:, :]], axis=2)


def solution(mesh):
    return jax.shard_map(
        body,
        mesh=mesh,
        in_specs=(P(None, "ax", "rad", "sec"), P()),
        out_specs=P(None, "ax", "rad", "sec"),
        check_vma=False,
    )
```

profile of v0, /device:TPU:6, one launch (start us, length us, event | category | flops | bytes accessed | tf_op | source)
XLA Modules:
  0.0 309.1 jit_solution(6789559779002969412)
XLA Ops:
  6.5 0.0 copy-start
  6.5 0.0 all-reduce.2.cloned.1.call-start
  6.5 1.3 fusion.47
  7.8 3.5 %collective-permute-start = (f32[5,2,64,1]{3,2,1,0:T(8,128)S(1)}, f32[5,2,64,1]{3,2,1,0:T(8,128)S(1)}, u32[]{:S(2)}, u32[]{:S(2)}) collective-permute-start(f32[5,2,64,1]{3,2,1,0:T(8,128)S(1)} %get-tuple-element.59), channel_id=1, source_target_pairs={{0,64},{64,128},{128,192},{192,256},{256,320},{320,384},{384,448},... | collective-permute-start | bytes 7688 | tf_op jit(solution)/shard_map/ppermute | solution.py:19
  11.3 3.8 %collective-permute-start.1 = (f32[5,2,64,1]{3,2,1,0:T(8,128)S(1)}, f32[5,2,64,1]{3,2,1,0:T(8,128)S(1)}, u32[]{:S(2)}, u32[]{:S(2)}) collective-permute-start(f32[5,2,64,1]{3,2,1,0:T(8,128)S(1)} %get-tuple-element.60), channel_id=1, source_target_pairs={{64,0},{128,64},{192,128},{256,192},{320,256},{384,320},{448,384},... | collective-permute-start | bytes 7688 | tf_op jit(solution)/shard_map/ppermute | solution.py:20
  15.2 0.1 broadcast_multiply_fusion.2
  15.2 1.4 fusion.44
  16.6 4.3 %collective-permute-done = f32[5,2,64,1]{3,2,1,0:T(8,128)S(1)} collective-permute-done((f32[5,2,64,1]{3,2,1,0:T(8,128)S(1)}, f32[5,2,64,1]{3,2,1,0:T(8,128)S(1)}, u32[]{:S(2)}, u32[]{:S(2)}) %collective-permute-start) | collective-permute-done | bytes 2592 | tf_op jit(solution)/shard_map/ppermute | solution.py:19
  20.9 1.5 collective-permute-done.1
  22.4 1.1 pad_maximum_fusion.5
  23.5 5.1 %collective-permute-start.2 = (f32[5,2,1,258]{3,2,1,0:T(1,128)S(1)}, f32[5,2,1,258]{3,2,1,0:T(1,128)S(1)}, u32[]{:S(2)}, u32[]{:S(2)}) collective-permute-start(f32[5,2,1,258]{3,2,1,0:T(1,128)S(1)} %get-tuple-element.53), channel_id=1, source_target_pairs={{0,4},{4,8},{8,12},{12,16},{16,20},{20,24},{24,28},{28,32},{32,36}... | collective-permute-start | bytes 30968 | tf_op jit(solution)/shard_map/ppermute | solution.py:19
  28.6 2.2 collective-permute-start.3
  30.9 0.0 collective-permute-done.2
  30.9 5.8 %collective-permute-done.3 = f32[5,2,1,258]{3,2,1,0:T(1,128)S(1)} collective-permute-done((f32[5,2,1,258]{3,2,1,0:T(1,128)S(1)}, f32[5,2,1,258]{3,2,1,0:T(1,128)S(1)}, u32[]{:S(2)}, u32[]{:S(2)}) %collective-permute-start.3) | collective-permute-done | bytes 10352 | tf_op jit(solution)/shard_map/ppermute | solution.py:20
  36.6 0.0 copy-done
  36.6 0.5 pad_maximum_fusion.1
  37.1 0.1 fusion.46
  37.2 0.5 copy.5
  37.7 1.9 collective-permute-start.4
  39.6 0.5 copy.6
  40.2 3.6 %collective-permute-start.5 = (f32[5,1,66,258]{3,1,2,0:T(1,128)S(1)}, f32[5,1,66,258]{3,1,2,0:T(1,128)S(1)}, u32[]{:S(2)}, u32[]{:S(2)}) collective-permute-start(f32[5,1,66,258]{3,1,2,0:T(1,128)S(1)} %copy.6), channel_id=1, source_target_pairs={{1,0},{2,1},{3,2},{0,3},{5,4},{6,5},{7,6},{4,7},{9,8},{10,9},{11,1... | collective-permute-start | bytes 1021688 | tf_op jit(solution)/shard_map/ppermute | solution.py:20
  43.9 0.1 pad.5.clone
  44.7 0.1 broadcast_add_fusion
  44.7 6.0 %collective-permute-done.4 = f32[5,1,66,258]{3,1,2,0:T(1,128)S(1)} collective-permute-done((f32[5,1,66,258]{3,1,2,0:T(1,128)S(1)}, f32[5,1,66,258]{3,1,2,0:T(1,128)S(1)}, u32[]{:S(2)}, u32[]{:S(2)}) %collective-permute-start.4) | collective-permute-done | bytes 340592 | tf_op jit(solution)/shard_map/ppermute | solution.py:19
  50.8 0.1 collective-permute-done.5
  51.0 0.5 pad_maximum_fusion
  51.5 0.2 slice_bitcast_fusion.3
  51.7 0.2 fusion.28
  51.9 0.3 add_dynamic-update-slice_fusion.2
  52.2 0.1 multiply_dynamic-update-slice_fusion.8
  52.2 0.1 multiply_dynamic-update-slice_fusion.7
  52.4 0.1 multiply_dynamic-update-slice_fusion.1
  52.4 0.1 add_dynamic-update-slice_fusion
  52.5 0.2 multiply_dynamic-update-slice_fusion.6
  52.7 0.1 multiply_dynamic-update-slice_fusion.4
  52.8 0.1 multiply_dynamic-update-slice_fusion.3
  52.9 0.4 broadcast_multiply_fusion
  53.3 0.3 fusion.32
  53.6 1.1 fusion.19
  54.7 0.7 slice_select_fusion.1
  55.4 0.0 all-reduce.2.cloned.1.call-update
  55.4 0.8 and_select_fusion
  58.5 0.8 add_select_fusion.1
  59.4 161.4 %all-reduce.2.cloned.1.call-done = f32[16,10,256]{2,0,1:T(8,128)} async-done(((f32[16,10,256]{2,0,1:T(8,128)}), f32[16,10,256]{2,0,1:T(8,128)}) %all-reduce.2.cloned.1.call-update) | async-done | bytes 163856 | tf_op jit(solution)/shard_map/psum | solution.py:27
  220.8 0.9 constant_dynamic-slice_fusion
  221.7 16.7 %all_gather.6 = f32[1,10,2048]{2,0,1:T(1,128)S(1)} all-gather(f32[1,10,256]{2,0,1:T(1,128)S(1)} %constant_dynamic-slice_fusion), channel_id=1, replica_groups=mesh['sec'=8,'rad'=16,'ax'=4] {'sec'}, dimensions={2}, use_global_device_ids=true | all-gather | bytes 92160 | tf_op jit(solution)/shard_map/all_gather | solution.py:153
  238.4 22.6 %fusion.7 = f32[1,10,256]{2,1,0:T(8,128)S(1)} fusion(f32[]{:T(128)S(6)} %mul.233, f32[]{:T(128)S(6)} %convert_element_type.66, f32[]{:T(128)} %bitcast.13, s32[]{:T(128)S(6)} %select_n.132, s32[2048]{0:T(1024)S(1)} %add_select_fusion.1, s32[256]{0:T(256)S(1)} %and_select_fusion, pred[]{:T(512)S(6)} %lt.63, f32[1,10,2048]{2,0,1:T(1,128)S(1)} %all_gather.6), kind=kOutput, calls=%fused_computation.10 | convolution fusion | flops 70254592 | bytes 101393 | tf_op jit(solution)/shard_map/while/body/eval_jaxpr/lq,pq->lp/dot_general | solution.py:159
  261.0 40.3 %all-gather.1 = f32[16,10,256]{2,1,0:T(8,128)S(1)} all-gather(f32[1,10,256]{2,1,0:T(8,128)S(1)} %fusion.7), channel_id=2, replica_groups=mesh['sec'=8,'rad'=16,'ax'=4] {'rad'}, dimensions={0}, use_global_device_ids=true | all-gather | bytes 174080 | tf_op jit(solution)/shard_map/all_gather | solution.py:162
  301.2 0.1 copy.9
  301.4 0.9 pad_maximum_fusion.2
  (12 shorter events, 0.2 us)
Async XLA Ops:
  6.5 30.1 %copy-start = (f32[5,2,64,256]{3,2,1,0:T(8,128)S(1)}, f32[5,2,64,256]{3,2,1,0:T(8,128)}, u32[]{:S(2)}) copy-start(f32[5,2,64,256]{3,2,1,0:T(8,128)} %param.2) | copy-start | bytes 1966084
  6.5 214.2 %all-reduce.2.cloned.1.call-start = ((), (), s32[]{:S(2)}) async-start(), calls=%async_computation | async-start | bytes 327680 | tf_op jit(solution)/shard_map/psum | solution.py:27
  7.8 13.1 %collective-permute-start = (f32[5,2,64,1]{3,2,1,0:T(8,128)S(1)}, f32[5,2,64,1]{3,2,1,0:T(8,128)S(1)}, u32[]{:S(2)}, u32[]{:S(2)}) collective-permute-start(f32[5,2,64,1]{3,2,1,0:T(8,128)S(1)} %get-tuple-element.59), channel_id=1, source_target_pairs={{0,64},{64,128},{128,192},{192,256},{256,320},{320,384},{384,448},... | collective-permute-start | bytes 7688 | tf_op jit(solution)/shard_map/ppermute | solution.py:19
  11.3 11.1 %collective-permute-start.1 = (f32[5,2,64,1]{3,2,1,0:T(8,128)S(1)}, f32[5,2,64,1]{3,2,1,0:T(8,128)S(1)}, u32[]{:S(2)}, u32[]{:S(2)}) collective-permute-start(f32[5,2,64,1]{3,2,1,0:T(8,128)S(1)} %get-tuple-element.60), channel_id=1, source_target_pairs={{64,0},{128,64},{192,128},{256,192},{320,256},{384,320},{448,384},... | collective-permute-start | bytes 7688 | tf_op jit(solution)/shard_map/ppermute | solution.py:20
  23.5 7.4 %collective-permute-start.2 = (f32[5,2,1,258]{3,2,1,0:T(1,128)S(1)}, f32[5,2,1,258]{3,2,1,0:T(1,128)S(1)}, u32[]{:S(2)}, u32[]{:S(2)}) collective-permute-start(f32[5,2,1,258]{3,2,1,0:T(1,128)S(1)} %get-tuple-element.53), channel_id=1, source_target_pairs={{0,4},{4,8},{8,12},{12,16},{16,20},{20,24},{24,28},{28,32},{32,36}... | collective-permute-start | bytes 30968 | tf_op jit(solution)/shard_map/ppermute | solution.py:19
  28.6 8.0 %collective-permute-start.3 = (f32[5,2,1,258]{3,2,1,0:T(1,128)S(1)}, f32[5,2,1,258]{3,2,1,0:T(1,128)S(1)}, u32[]{:S(2)}, u32[]{:S(2)}) collective-permute-start(f32[5,2,1,258]{3,2,1,0:T(1,128)S(1)} %get-tuple-element.54), channel_id=1, source_target_pairs={{4,0},{8,4},{12,8},{16,12},{20,16},{24,20},{28,24},{32,28},{36,32}... | collective-permute-start | bytes 30968 | tf_op jit(solution)/shard_map/ppermute | solution.py:20
  37.7 13.0 %collective-permute-start.4 = (f32[5,1,66,258]{3,1,2,0:T(1,128)S(1)}, f32[5,1,66,258]{3,1,2,0:T(1,128)S(1)}, u32[]{:S(2)}, u32[]{:S(2)}) collective-permute-start(f32[5,1,66,258]{3,1,2,0:T(1,128)S(1)} %copy.5), channel_id=1, source_target_pairs={{0,1},{1,2},{2,3},{3,0},{4,5},{5,6},{6,7},{7,4},{8,9},{9,10},{10,1... | collective-permute-start | bytes 1021688 | tf_op jit(solution)/shard_map/ppermute | solution.py:19
  40.2 10.7 %collective-permute-start.5 = (f32[5,1,66,258]{3,1,2,0:T(1,128)S(1)}, f32[5,1,66,258]{3,1,2,0:T(1,128)S(1)}, u32[]{:S(2)}, u32[]{:S(2)}) collective-permute-start(f32[5,1,66,258]{3,1,2,0:T(1,128)S(1)} %copy.6), channel_id=1, source_target_pairs={{1,0},{2,1},{3,2},{0,3},{5,4},{6,5},{7,6},{4,7},{9,8},{10,9},{11,1... | collective-permute-start | bytes 1021688 | tf_op jit(solution)/shard_map/ppermute | solution.py:20
Sparse Core Ops, SparseCore 0:
  55.5 165.2 all-reduce.1
where the time goes:
time: 310 us; the launch traced here: 309 us
  waiting for transfers between devices  179 us (58%)
  blocking collectives  57 us (18%)
  matrix products  22.6 us (7%)
  starting transfers between devices  20.2 us (7%)
  between operations  16.7 us (5%)
  other arithmetic  9.79 us (3%)
  local copies, waits for them, and re-layouts  3.82 us (1%)
    psum x1, waiting for transfers between devices, spread(): return lax.psum(jnp.where(mine, value, jnp.zeros_like(value)), axis)  161 us
    all_gather x1, blocking collectives, body(): result = lax.all_gather(smoothed, 'rad', axis=0, tiled=True)  40.3 us
    dot_general x1, matrix products, per_cycle(): jnp.einsum('lq,pq->lp', lines_one, table, precision=lax.Precision.HIGHEST)  22.6 us
    all_gather x1, blocking collectives, body(): portion = lax.all_gather(my_cycles, 'sec', axis=2, tiled=True)  16.7 us
    ppermute x3, starting transfers between devices, padded_2(): before = lax.ppermute(last, axis, up)  10.5 us
    ppermute x3, waiting for transfers between devices, padded_2(): before = lax.ppermute(last, axis, up)  10.3 us
    ppermute x3, starting transfers between devices, padded_2(): after = lax.ppermute(first, axis, down)  9.68 us
    ppermute x3, waiting for transfers between devices, padded_2(): after = lax.ppermute(first, axis, down)  7.38 us
  transfers between devices with their start and end apart: 7, of which 6 were waited for; matrix products, arithmetic and copies ran while one was open for 1% of the time, Pallas kernels for 0%

commit v1 on v0

--- a/solution.py
+++ b/solution.py
@@ -24,7 +24,7 @@
 
 def spread(value, axis, root):
     mine = lax.axis_index(axis) == root
-    return lax.psum(jnp.where(mine, value, jnp.zeros_like(value)), axis)
+    return jnp.sum(lax.all_gather(jnp.where(mine, value, jnp.zeros_like(value)), axis), axis=0)
 
 
 def body(state, coarsen):

time: 310 us -> 245 us (0.79)
  waiting for transfers between devices: 179 us -> 115 us
    psum x1 -> x0, waiting for transfers between devices: 161 us -> none  [spread(): return lax.psum(jnp.where(mine, value, jnp.zeros_like(value)), axis)]
    all_gather x0 -> x1, waiting for transfers between devices: none -> 95.5 us  [spread(): lax.all_gather(jnp.where(mine, value, jnp.zeros_like(value)), axis)]
where the time goes in v1:
time: 245 us; the launch traced here: 244 us
  waiting for transfers between devices  115 us (47%)
  blocking collectives  55.9 us (23%)
  matrix products  22.5 us (9%)
  starting transfers between devices  20.2 us (8%)
  between operations  16.1 us (7%)
  other arithmetic  10.8 us (4%)
  local copies, waits for them, and re-layouts  2.94 us (1%)
    all_gather x1, waiting for transfers between devices, spread(): lax.all_gather(jnp.where(mine, value, jnp.zeros_like(value)), axis)  95.5 us
    all_gather x1, blocking collectives, body(): result = lax.all_gather(smoothed, 'rad', axis=0, tiled=True)  39.2 us
    dot_general x1, matrix products, per_cycle(): jnp.einsum('lq,pq->lp', lines_one, table, precision=lax.Precision.HIGHEST)  22.5 us
    all_gather x1, blocking collectives, body(): portion = lax.all_gather(my_cycles, 'sec', axis=2, tiled=True)  16.8 us
    ppermute x3, waiting for transfers between devices, padded_2(): before = lax.ppermute(last, axis, up)  12.4 us
    ppermute x3, starting transfers between devices, padded_2(): before = lax.ppermute(last, axis, up)  10.5 us
    ppermute x3, starting transfers between devices, padded_2(): after = lax.ppermute(first, axis, down)  9.68 us
    ppermute x3, waiting for transfers between devices, padded_2(): after = lax.ppermute(first, axis, down)  7.38 us
  transfers between devices with their start and end apart: 7, of which 6 were waited for; matrix products, arithmetic and copies ran while one was open for 1% of the time, Pallas kernels for 0%

profile of v1, /device:TPU:6, one launch (start us, length us, event | category | flops | bytes accessed | tf_op | source)
XLA Modules:
  0.0 243.8 jit_solution(2670346385443575479)
XLA Ops:
  6.5 0.0 copy-start
  6.5 0.0 all-gather.4.cloned.1.call-start
  6.5 1.3 fusion.47
  7.8 3.5 %collective-permute-start = (f32[5,2,64,1]{3,2,1,0:T(8,128)S(1)}, f32[5,2,64,1]{3,2,1,0:T(8,128)S(1)}, u32[]{:S(2)}, u32[]{:S(2)}) collective-permute-start(f32[5,2,64,1]{3,2,1,0:T(8,128)S(1)} %get-tuple-element.59), channel_id=1, source_target_pairs={{0,64},{64,128},{128,192},{192,256},{256,320},{320,384},{384,448},... | collective-permute-start | bytes 7688 | tf_op jit(solution)/shard_map/ppermute | solution.py:19
  11.3 3.8 %collective-permute-start.1 = (f32[5,2,64,1]{3,2,1,0:T(8,128)S(1)}, f32[5,2,64,1]{3,2,1,0:T(8,128)S(1)}, u32[]{:S(2)}, u32[]{:S(2)}) collective-permute-start(f32[5,2,64,1]{3,2,1,0:T(8,128)S(1)} %get-tuple-element.60), channel_id=1, source_target_pairs={{64,0},{128,64},{192,128},{256,192},{320,256},{384,320},{448,384},... | collective-permute-start | bytes 7688 | tf_op jit(solution)/shard_map/ppermute | solution.py:20
  15.2 0.1 broadcast_multiply_fusion.2
  15.3 5.6 %collective-permute-done = f32[5,2,64,1]{3,2,1,0:T(8,128)S(1)} collective-permute-done((f32[5,2,64,1]{3,2,1,0:T(8,128)S(1)}, f32[5,2,64,1]{3,2,1,0:T(8,128)S(1)}, u32[]{:S(2)}, u32[]{:S(2)}) %collective-permute-start) | collective-permute-done | bytes 2592 | tf_op jit(solution)/shard_map/ppermute | solution.py:19
  20.9 1.5 collective-permute-done.1
  22.4 1.1 pad_maximum_fusion.5
  23.5 5.1 %collective-permute-start.2 = (f32[5,2,1,258]{3,2,1,0:T(1,128)S(1)}, f32[5,2,1,258]{3,2,1,0:T(1,128)S(1)}, u32[]{:S(2)}, u32[]{:S(2)}) collective-permute-start(f32[5,2,1,258]{3,2,1,0:T(1,128)S(1)} %get-tuple-element.53), channel_id=1, source_target_pairs={{0,4},{4,8},{8,12},{12,16},{16,20},{20,24},{24,28},{28,32},{32,36}... | collective-permute-start | bytes 30968 | tf_op jit(solution)/shard_map/ppermute | solution.py:19
  28.6 2.2 collective-permute-start.3
  30.9 0.0 collective-permute-done.2
  30.9 5.8 %collective-permute-done.3 = f32[5,2,1,258]{3,2,1,0:T(1,128)S(1)} collective-permute-done((f32[5,2,1,258]{3,2,1,0:T(1,128)S(1)}, f32[5,2,1,258]{3,2,1,0:T(1,128)S(1)}, u32[]{:S(2)}, u32[]{:S(2)}) %collective-permute-start.3) | collective-permute-done | bytes 10352 | tf_op jit(solution)/shard_map/ppermute | solution.py:20
  36.6 0.0 copy-done
  36.6 0.5 pad_maximum_fusion.1
  37.1 0.1 fusion.46
  37.2 0.5 copy.5
  37.7 1.9 collective-permute-start.4
  39.6 0.5 copy.6
  40.2 3.6 %collective-permute-start.5 = (f32[5,1,66,258]{3,1,2,0:T(1,128)S(1)}, f32[5,1,66,258]{3,1,2,0:T(1,128)S(1)}, u32[]{:S(2)}, u32[]{:S(2)}) collective-permute-start(f32[5,1,66,258]{3,1,2,0:T(1,128)S(1)} %copy.6), channel_id=1, source_target_pairs={{1,0},{2,1},{3,2},{0,3},{5,4},{6,5},{7,6},{4,7},{9,8},{10,9},{11,1... | collective-permute-start | bytes 1021688 | tf_op jit(solution)/shard_map/ppermute | solution.py:20
  43.9 0.1 pad.5.clone
  43.9 0.1 broadcast_add_fusion
  44.0 6.7 %collective-permute-done.4 = f32[5,1,66,258]{3,1,2,0:T(1,128)S(1)} collective-permute-done((f32[5,1,66,258]{3,1,2,0:T(1,128)S(1)}, f32[5,1,66,258]{3,1,2,0:T(1,128)S(1)}, u32[]{:S(2)}, u32[]{:S(2)}) %collective-permute-start.4) | collective-permute-done | bytes 340592 | tf_op jit(solution)/shard_map/ppermute | solution.py:19
  50.8 0.1 collective-permute-done.5
  50.9 0.5 pad_maximum_fusion
  51.4 0.2 slice_bitcast_fusion.3
  51.7 0.2 fusion.28
  51.9 0.3 add_dynamic-update-slice_fusion.2
  52.2 0.1 multiply_dynamic-update-slice_fusion.8
  52.2 0.1 multiply_dynamic-update-slice_fusion.7
  52.4 0.1 multiply_dynamic-update-slice_fusion.1
  52.4 0.1 add_dynamic-update-slice_fusion
  52.5 0.2 multiply_dynamic-update-slice_fusion.6
  52.7 0.1 multiply_dynamic-update-slice_fusion.4
  52.8 0.1 multiply_dynamic-update-slice_fusion.3
  52.8 0.4 broadcast_multiply_fusion
  53.3 0.3 fusion.32
  53.6 0.0 copy-start.1
  53.6 1.1 fusion.19
  54.7 0.7 slice_select_fusion.1
  55.4 0.0 all-gather.4.cloned.1.call-update
  55.4 0.0 copy-done.1
  55.4 0.6 fusion.44
  58.5 0.7 and_select_fusion
  59.2 0.7 add_select_fusion.1
  59.9 95.5 %all-gather.4.cloned.1.call-done = f32[16,16,10,256]{3,1,2,0:T(8,128)} async-done(((f32[1,16,10,256]{3,1,2,0:T(8,128)}), f32[16,16,10,256]{3,1,2,0:T(8,128)}) %all-gather.4.cloned.1.call-update) | async-done | bytes 2621456 | tf_op jit(solution)/shard_map/all_gather | solution.py:27
  155.5 2.0 reduce_sum.18
  157.5 16.8 %all_gather.11 = f32[1,10,2048]{2,0,1:T(1,128)S(1)} all-gather(f32[1,10,256]{2,0,1:T(1,128)S(1)} %constant_dynamic-slice_fusion), channel_id=1, replica_groups=mesh['sec'=8,'rad'=16,'ax'=4] {'sec'}, dimensions={2}, use_global_device_ids=true | all-gather | bytes 92160 | tf_op jit(solution)/shard_map/all_gather | solution.py:153
  174.2 22.5 %fusion.7 = f32[1,10,256]{2,1,0:T(8,128)S(1)} fusion(f32[]{:T(128)S(6)} %mul.233, f32[]{:T(128)S(6)} %convert_element_type.66, f32[]{:T(128)} %bitcast.13, s32[]{:T(128)S(6)} %select_n.139, s32[2048]{0:T(1024)S(1)} %add_select_fusion.1, s32[256]{0:T(256)S(1)} %and_select_fusion, pred[]{:T(512)S(6)} %lt.63, f32[1,10,2048]{2,0,1:T(1,128)S(1)} %all_gather.11), kind=kOutput, calls=%fused_computation.10 | convolution fusion | flops 70254592 | bytes 101393 | tf_op jit(solution)/shard_map/while/body/eval_jaxpr/lq,pq->lp/dot_general | solution.py:159
  196.8 39.2 %all-gather.1 = f32[16,10,256]{2,1,0:T(8,128)S(1)} all-gather(f32[1,10,256]{2,1,0:T(8,128)S(1)} %fusion.7), channel_id=2, replica_groups=mesh['sec'=8,'rad'=16,'ax'=4] {'rad'}, dimensions={0}, use_global_device_ids=true | all-gather | bytes 174080 | tf_op jit(solution)/shard_map/all_gather | solution.py:162
  235.9 0.1 copy.9
  236.1 0.9 pad_maximum_fusion.2
  (13 shorter events, 0.2 us)
Async XLA Ops:
  6.5 30.1 %copy-start = (f32[5,2,64,256]{3,2,1,0:T(8,128)S(1)}, f32[5,2,64,256]{3,2,1,0:T(8,128)}, u32[]{:S(2)}) copy-start(f32[5,2,64,256]{3,2,1,0:T(8,128)} %param.2) | copy-start | bytes 1966084
  6.5 148.9 %all-gather.4.cloned.1.call-start = ((), (), s32[]{:S(2)}) async-start(), calls=%async_computation | async-start | bytes 2785280 | tf_op jit(solution)/shard_map/all_gather | solution.py:27
  7.8 13.1 %collective-permute-start = (f32[5,2,64,1]{3,2,1,0:T(8,128)S(1)}, f32[5,2,64,1]{3,2,1,0:T(8,128)S(1)}, u32[]{:S(2)}, u32[]{:S(2)}) collective-permute-start(f32[5,2,64,1]{3,2,1,0:T(8,128)S(1)} %get-tuple-element.59), channel_id=1, source_target_pairs={{0,64},{64,128},{128,192},{192,256},{256,320},{320,384},{384,448},... | collective-permute-start | bytes 7688 | tf_op jit(solution)/shard_map/ppermute | solution.py:19
  11.3 11.1 %collective-permute-start.1 = (f32[5,2,64,1]{3,2,1,0:T(8,128)S(1)}, f32[5,2,64,1]{3,2,1,0:T(8,128)S(1)}, u32[]{:S(2)}, u32[]{:S(2)}) collective-permute-start(f32[5,2,64,1]{3,2,1,0:T(8,128)S(1)} %get-tuple-element.60), channel_id=1, source_target_pairs={{64,0},{128,64},{192,128},{256,192},{320,256},{384,320},{448,384},... | collective-permute-start | bytes 7688 | tf_op jit(solution)/shard_map/ppermute | solution.py:20
  23.5 7.4 %collective-permute-start.2 = (f32[5,2,1,258]{3,2,1,0:T(1,128)S(1)}, f32[5,2,1,258]{3,2,1,0:T(1,128)S(1)}, u32[]{:S(2)}, u32[]{:S(2)}) collective-permute-start(f32[5,2,1,258]{3,2,1,0:T(1,128)S(1)} %get-tuple-element.53), channel_id=1, source_target_pairs={{0,4},{4,8},{8,12},{12,16},{16,20},{20,24},{24,28},{28,32},{32,36}... | collective-permute-start | bytes 30968 | tf_op jit(solution)/shard_map/ppermute | solution.py:19
  28.6 8.0 %collective-permute-start.3 = (f32[5,2,1,258]{3,2,1,0:T(1,128)S(1)}, f32[5,2,1,258]{3,2,1,0:T(1,128)S(1)}, u32[]{:S(2)}, u32[]{:S(2)}) collective-permute-start(f32[5,2,1,258]{3,2,1,0:T(1,128)S(1)} %get-tuple-element.54), channel_id=1, source_target_pairs={{4,0},{8,4},{12,8},{16,12},{20,16},{24,20},{28,24},{32,28},{36,32}... | collective-permute-start | bytes 30968 | tf_op jit(solution)/shard_map/ppermute | solution.py:20
  37.7 13.0 %collective-permute-start.4 = (f32[5,1,66,258]{3,1,2,0:T(1,128)S(1)}, f32[5,1,66,258]{3,1,2,0:T(1,128)S(1)}, u32[]{:S(2)}, u32[]{:S(2)}) collective-permute-start(f32[5,1,66,258]{3,1,2,0:T(1,128)S(1)} %copy.5), channel_id=1, source_target_pairs={{0,1},{1,2},{2,3},{3,0},{4,5},{5,6},{6,7},{7,4},{8,9},{9,10},{10,1... | collective-permute-start | bytes 1021688 | tf_op jit(solution)/shard_map/ppermute | solution.py:19
  40.2 10.7 %collective-permute-start.5 = (f32[5,1,66,258]{3,1,2,0:T(1,128)S(1)}, f32[5,1,66,258]{3,1,2,0:T(1,128)S(1)}, u32[]{:S(2)}, u32[]{:S(2)}) collective-permute-start(f32[5,1,66,258]{3,1,2,0:T(1,128)S(1)} %copy.6), channel_id=1, source_target_pairs={{1,0},{2,1},{3,2},{0,3},{5,4},{6,5},{7,6},{4,7},{9,8},{10,9},{11,1... | collective-permute-start | bytes 1021688 | tf_op jit(solution)/shard_map/ppermute | solution.py:20
  53.6 1.8 copy-start.1
Sparse Core Ops, SparseCore 0:
  55.5 99.8 all-gather.3
